TPU v7x, 32 devices: a whole 2x2x4 slice. The times are simulated.
32 devices in a mesh: seq: 16 (over z, y, x), head: 2 (over core).
Axes of the slice: x: 2, y: 2, z: 4, core: 2. Of those that a mesh axis runs over, the one named last changes fastest.
Arguments:
- tokens: float32 [2, 4096, 768], P(None, 'seq'), may hold values from -6 to 6
- norm_gain: float32 [768], replicated, may hold values from 0.5 to 1.5
- w_gate: float32 [768, 1536], P(None, 'head'), may hold values from -0.21875 to 0.21875
- w_inner: float32 [768, 1536], P(None, 'head'), may hold values from -0.21875 to 0.21875
- w_state: float32 [768, 256], replicated, may hold values from -0.21875 to 0.21875
- w_step: float32 [768, 24], P(None, 'head'), may hold values from -0.21875 to 0.21875
- conv_inner: float32 [4, 1536], P(None, 'head'), may hold values from -3 to 3
- conv_state: float32 [4, 256], replicated, may hold values from -3 to 3
- bias_inner: float32 [1536], P('head'), may hold values from -3 to 3
- bias_state: float32 [256], replicated, may hold values from -3 to 3
- step_bias: float32 [24], P('head'), may hold values from -4 to -2
- decay_log: float32 [24], P('head'), may hold values from -7.5 to 0
- skip_gain: float32 [24], P('head'), may hold values from 0.5 to 1.5
- out_gain: float32 [1536], P('head'), may hold values from 0.5 to 1.5
- w_out: float32 [1536, 768], P('head'), may hold values from -0.15625 to 0.15625
- cotangent: float32 [2, 4096, 768], P(None, 'seq', 'head'), may hold values from -6 to 6
Outputs:
- result: float32 [2, 4096, 768], P(None, 'seq', 'head')
- grad_tokens: float32 [2, 4096, 768], P(None, 'seq', 'head')
- grad_norm_gain: float32 [768], replicated
- grad_w_gate: float32 [768, 1536], P(None, 'head')
- grad_w_inner: float32 [768, 1536], P(None, 'head')
- grad_w_state: float32 [768, 256], replicated
- grad_w_step: float32 [768, 24], P(None, 'head')
- grad_conv_inner: float32 [4, 1536], P(None, 'head')
- grad_conv_state: float32 [4, 256], replicated
- grad_bias_inner: float32 [1536], P('head')
- grad_bias_state: float32 [256], replicated
- grad_step_bias: float32 [24], P('head')
- grad_decay_log: float32 [24], P('head')
- grad_skip_gain: float32 [24], P('head')
- grad_out_gain: float32 [1536], P('head')
- grad_w_out: float32 [1536, 768], P('head')
All inputs are finite; a program needn't handle non-finite values.
Results may differ from a plain program's by a relative error of at most 0.0003.
Values sent between devices are 32-bit elements; how exact they have to be, the bound alone decides.
A program may use at most 256 MiB of HBM per device.

v0:
```python
import jax
import jax.numpy as jnp
from jax import lax
from jax.sharding import PartitionSpec as P

HEADS = 24
HEAD_DIM = 64
STATE = 128


highest = lax.Precision.HIGHEST
epsilon = 1e-05


def shifted(array, axis, by):
    length = lax.axis_size(axis)
    pairs = [(i, i + by) for i in range(length) if 0 <= i + by < length]
    return lax.ppermute(array, axis, pairs)


def entering_2(array, axis, combine, identity, reverse):
    length, index = (lax.axis_size(axis), lax.axis_index(axis))
    everything = jax.tree.map(lambda part: lax.all_gather(part, axis), array)
    start = jax.tree.map(
        lambda part, zero: jnp.broadcast_to(jnp.asarray(zero, part.dtype), part.shape),
        array,
        identity,
    )

    def hop(k, before):
        at = length - 1 - k if reverse else k
        reached = at > index if reverse else at < index
        new = combine(before, jax.tree.map(lambda part: part[at], everything))
        return jax.tree.map(lambda a, b: jnp.where(reached, a, b), new, before)

    return lax.fori_loop(0, length, hop, start)


def product(left, right):
    return jnp.einsum("...k,kn->...n", left, right, precision=highest)


def normalize(tokens, norm_gain):
    inverse = lax.rsqrt(jnp.mean(tokens * tokens, axis=-1, keepdims=True) + epsilon)
    return tokens * inverse * norm_gain


def project(hidden, w_gate, w_inner, w_state, w_step):
    mixed_in = jnp.concatenate([product(hidden, w_inner), product(hidden, w_state)], axis=-1)
    return (product(hidden, w_gate), mixed_in, product(hidden, w_step))


def convolve(
    mixed_in, before, conv_inner, conv_state, bias_inner, bias_state, raw_step, step_bias, decay_log
):
    weights = jnp.concatenate([conv_inner, conv_state], axis=-1)
    summed = jnp.concatenate([bias_inner, bias_state], axis=-1) + jnp.zeros_like(mixed_in)
    padded = jnp.concatenate([before, mixed_in], axis=1)
    length = mixed_in.shape[1]
    for offset in range(weights.shape[0]):
        summed = summed + weights[offset] * padded[:, offset : offset + length]
    step_size = jax.nn.softplus(raw_step + step_bias)
    cumulative = jnp.cumsum(-jnp.exp(decay_log) * step_size, axis=1)
    return (jax.nn.silu(summed), step_size, cumulative)


def unpack(active):
    inner_width = active.shape[-1] - 2 * STATE
    inner_x = active[..., :inner_width].reshape(
        active.shape[0], active.shape[1], inner_width // HEAD_DIM, HEAD_DIM
    )
    return (
        inner_x,
        active[..., inner_width : inner_width + STATE],
        active[..., inner_width + STATE :],
    )


def end_state(active, step_size, cumulative):
    inner_x, input_map, output_map = unpack(active)
    weight_end = jnp.exp(cumulative[:, -1:, :] - cumulative) * step_size
    local_state = jnp.einsum(
        "slh,slhp,sln->shpn", weight_end, inner_x, input_map, precision=highest
    )
    return (local_state, jnp.exp(cumulative[:, -1, :]))


def group_out(active, step_size, cumulative, entering, gate_proj, skip_gain):
    inner_x, input_map, output_map = unpack(active)
    length = active.shape[1]
    scores = jnp.einsum("stn,srn->str", output_map, input_map, precision=highest)
    by_head = jnp.transpose(cumulative, (0, 2, 1))
    causal = (jnp.arange(length)[:, None] >= jnp.arange(length)[None, :])[None, None]
    spread = by_head[:, :, :, None] - by_head[:, :, None, :]
    decays = jnp.where(causal, jnp.exp(jnp.where(causal, spread, 0.0)), 0.0)
    mixing = scores[:, None] * decays * jnp.transpose(step_size, (0, 2, 1))[:, :, None, :]
    within = jnp.einsum("shtr,srhp->sthp", mixing, inner_x, precision=highest)
    across = jnp.exp(cumulative)[..., None] * jnp.einsum(
        "stn,shpn->sthp", output_map, entering, precision=highest
    )
    output = within + across + skip_gain[:, None] * inner_x
    gated_out = output.reshape(gate_proj.shape) * jax.nn.silu(gate_proj)
    return (gated_out, jnp.sum(gated_out * gated_out, axis=-1))


def finish(gated_out, square_sum, out_gain, w_out):
    inverse = lax.rsqrt(square_sum / (HEADS * HEAD_DIM) + epsilon)
    return product(gated_out * inverse[..., None] * out_gain, w_out)


def combine_state(earlier, later):
    return (earlier[0] * later[0], earlier[1] * later[0][:, :, None, None] + later[1])


def body(
    tokens,
    norm_gain,
    w_gate,
    w_inner,
    w_state,
    w_step,
    conv_inner,
    conv_state,
    bias_inner,
    bias_state,
    step_bias,
    decay_log,
    skip_gain,
    out_gain,
    w_out,
    cotangent,
):
    hidden, norm_back = jax.vjp(normalize, tokens, norm_gain)
    (gate_proj, mixed_in, raw_step), project_back = jax.vjp(
        project, hidden, w_gate, w_inner, w_state, w_step
    )
    edge_rows = conv_inner.shape[0] - 1
    before = shifted(mixed_in[:, mixed_in.shape[1] - edge_rows :], "seq", 1)
    (active, step_size, cumulative), convolve_back = jax.vjp(
        convolve,
        mixed_in,
        before,
        conv_inner,
        conv_state,
        bias_inner,
        bias_state,
        raw_step,
        step_bias,
        decay_log,
    )
    (local_state, decay_all), state_back = jax.vjp(end_state, active, step_size, cumulative)
    identity = (jnp.ones_like(decay_all), jnp.zeros_like(local_state))
    entering = entering_2((decay_all, local_state), "seq", combine_state, identity, False)[1]
    (gated_out, partial_sq), group_back = jax.vjp(
        group_out, active, step_size, cumulative, entering, gate_proj, skip_gain
    )
    square_sum = lax.psum(partial_sq, "head")
    partial_out, finish_back = jax.vjp(finish, gated_out, square_sum, out_gain, w_out)
    shared_out = lax.psum_scatter(partial_out, "head", scatter_dimension=2, tiled=True)
    columns = shared_out.shape[2]
    col_start = lax.axis_index("head") * columns
    result = lax.dynamic_slice_in_dim(tokens, col_start, columns, 2) + shared_out
    full_cot = lax.all_gather(cotangent, "head", axis=2, tiled=True)
    grad_gated, grad_square, grad_out_gain, grad_w_out = finish_back(full_cot)
    grad_partial_sq = lax.psum(grad_square, "head")
    grad_active, grad_step, grad_cumul, grad_entering, grad_gate, grad_skip_gain = group_back(
        (grad_gated, grad_partial_sq)
    )
    carried = entering_2((decay_all, grad_entering), "seq", combine_state, identity, True)[1]
    grad_decay = jnp.sum(carried * entering, axis=(2, 3))
    more_active, more_step, more_cumul = state_back((carried, grad_decay))
    grad_active = grad_active + more_active
    grad_step = grad_step + more_step
    grad_cumul = grad_cumul + more_cumul
    (
        grad_mixed,
        grad_before,
        grad_conv_inner,
        grad_conv_state,
        grad_bias_inner,
        grad_bias_state,
        grad_raw,
        grad_step_bias,
        grad_decay_log,
    ) = convolve_back((grad_active, grad_step, grad_cumul))
    returned = shifted(grad_before, "seq", -1)
    grad_mixed = grad_mixed.at[:, grad_mixed.shape[1] - edge_rows :].add(returned)
    grad_hidden, grad_w_gate, grad_w_inner, grad_w_state, grad_w_step = project_back(
        (grad_gate, grad_mixed, grad_raw)
    )
    whole_hidden = lax.psum(grad_hidden, "head")
    whole_tokens, grad_norm_gain = norm_back(whole_hidden)
    grad_tokens = cotangent + lax.dynamic_slice_in_dim(whole_tokens, col_start, columns, 2)
    head_sums = lax.psum(
        (
            grad_w_gate,
            grad_w_inner,
            grad_w_step,
            grad_conv_inner,
            grad_bias_inner,
            grad_step_bias,
            grad_decay_log,
            grad_skip_gain,
            grad_out_gain,
            grad_w_out,
            grad_norm_gain,
        ),
        "seq",
    )
    shared_sums = lax.psum((grad_w_state, grad_conv_state, grad_bias_state), ("seq", "head"))
    norm_total = head_sums[10]
    return (
        result,
        grad_tokens,
        norm_total,
        head_sums[0],
        head_sums[1],
        shared_sums[0],
        head_sums[2],
        head_sums[3],
        shared_sums[1],
        head_sums[4],
        shared_sums[2],
        head_sums[5],
        head_sums[6],
        head_sums[7],
        head_sums[8],
        head_sums[9],
    )


def solution(mesh):
    return jax.shard_map(
        body,
        mesh=mesh,
        in_specs=(
            P(None, "seq", None),
            P(),
            P(None, "head"),
            P(None, "head"),
            P(),
            P(None, "head"),
            P(None, "head"),
            P(),
            P("head"),
            P(),
            P("head"),
            P("head"),
            P("head"),
            P("head"),
            P("head", None),
            P(None, "seq", "head"),
        ),
        out_specs=(
            P(None, "seq", "head"),
            P(None, "seq", "head"),
            P(),
            P(None, "head"),
            P(None, "head"),
            P(),
            P(None, "head"),
            P(None, "head"),
            P(),
            P("head"),
            P(),
            P("head"),
            P("head"),
            P("head"),
            P("head"),
            P("head", None),
        ),
        check_vma=False,
    )
```

profile of v0, /device:TPU:0, one launch (start us, length us, event | category | flops | bytes accessed | tf_op | source)
XLA Modules:
  0.0 910.8 jit_solution(14638526698007550832)
XLA Ops:
  7.3 1.7 multiply_reduce_fusion.14
  9.6 2.8 fusion.73
  12.4 4.1 fusion.33
  18.3 5.6 collective-permute-start
  24.0 1.6 fusion.103
  29.5 1.6 bitcast_exponential_fusion
  32.2 1.8 maximum_maximum_fusion
  34.1 2.5 fusion.37
  39.2 3.0 copy.165
  42.2 3.8 fusion.60
  48.1 1.7 copy.172
  49.8 38.9 %all-gather = f32[32,1,12]{2,1,0:T(1,128)S(1)} all-gather(f32[2,1,12]{2,1,0:T(1,128)S(1)} %bitcast.222), channel_id=2, replica_groups=mesh['seq'=16,'head'=2] {'seq'}, dimensions={0}, use_global_device_ids=true | all-gather | bytes 1632 | tf_op jit(solution)/shard_map/all_gather | solution.py:23
  89.7 2.5 fusion.107
  92.2 105.9 %all-gather.9.cloned.1.call-done = f32[32,12,64,128]{3,2,1,0:T(8,128)} async-done(((f32[2,12,64,128]{3,2,1,0:T(8,128)}), f32[32,12,64,128]{3,2,1,0:T(8,128)}) %all-gather.9.cloned.1.call-update) | async-done | bytes 12582928 | tf_op jit(solution)/shard_map/all_gather | solution.py:23
  198.1 21.6 %while.31 = (s32[]{:T(128)}, f32[2,12,64,128]{3,2,1,0:T(8,128)S(1)}, s32[]{:T(128)}, f32[16,2,12]{2,1,0:T(2,128)S(1)}, f32[16,2,12,64,128]{4,3,2,1,0:T(8,128)}, /*index=5*/s32[]{:T(128)}, s32[]{:T(128)}) while((s32[]{:T(128)}, f32[2,12,64,128]{3,2,1,0:T(8,128)S(1)}, s32[]{:T(128)}, f32[16,2,12]{2,1,0:T(2,128)S(1)}, ...), condition=%wide.region_4.5_spmd.clone, body=%wide.region_3.4_spmd.clone.sunk | while | flops 786436 | bytes 2359697 | solution.py:36
  219.8 2.7 fusion.94
  222.5 8.5 fusion.40
  231.0 3.0 copy.177
  234.0 7.8 multiply_reduce_fusion.13
  241.8 2.7 psum.119
  244.5 8.5 multiply_reduce_fusion.7
  253.0 2.5 psum.120
  255.5 6.7 multiply_reduce_fusion.8
  262.1 3.1 copy.178
  265.2 3.8 fusion.54
  269.6 2.8 multiply_reduce_fusion.11
  272.4 1.6 copy.180
  274.0 13.0 %fusion.10 = (f32[2,12,256]{2,1,0:T(8,128)}, f32[2,12,256]{2,1,0:T(8,128)}, f32[2,12,256]{2,1,0:T(8,128)}, f32[2,256,256]{2,1,0:T(8,128)}) fusion(f32[2,12,256]{2,1,0:T(8,128)} %copy.172, f32[2,12,256]{2,1,0:T(8,128)} %copy.170, f32[2,256,256]{2,1,0:T(8,128)} %fusion.107, pred[256,256]{1,0:T(8,128)(4,1)} %iota_compare_fusion, ...), kind=kOutput, calls=%fused_computation.16 | convolution fusion | flops 1231403008 | bytes 4382720 | tf_op jit(solution)/shard_map/transpose(jvp(shtr,srhp->sthp))/dot_general | solution.py:97
  286.9 1.6 copy.181
  288.6 1.6 copy.182
  290.2 1.6 copy.179
  291.8 8.7 bitcast_add_fusion.2
  300.5 3.1 copy.190
  303.6 4.3 fusion.67
  307.9 2.8 fusion.110
  310.7 2.3 convolution_add_fusion
  313.0 5.2 fusion.27
  318.2 101.3 %all-gather.11.cloned.1.call-done = f32[32,12,64,128]{3,2,1,0:T(8,128)} async-done(((f32[2,12,64,128]{3,2,1,0:T(8,128)}), f32[32,12,64,128]{3,2,1,0:T(8,128)}) %all-gather.11.cloned.1.call-update) | async-done | bytes 12582928 | tf_op jit(solution)/shard_map/all_gather | solution.py:23
  419.6 22.1 %while.32 = (s32[]{:T(128)}, f32[2,12,64,128]{3,2,1,0:T(8,128)S(1)}, s32[]{:T(128)}, f32[16,2,12]{2,1,0:T(2,128)S(1)}, f32[16,2,12,64,128]{4,3,2,1,0:T(8,128)}, ...) while((s32[]{:T(128)}, f32[2,12,64,128]{3,2,1,0:T(8,128)S(1)}, s32[]{:T(128)}, ...), condition=%wide.region_12.13_spmd.clone, body=%wide.region_11.12_spmd.clone.sunk | while | flops 786440 | bytes 2359759 | solution.py:36
  443.1 3.6 multiply_reduce_fusion.6
  446.7 3.4 fusion.64
  450.1 3.1 copy.191
  454.8 5.0 reduce-window.16
  460.9 3.3 fusion.124
  465.3 2.6 fusion.114
  468.0 3.9 multiply_reduce_fusion.4
  473.0 1.5 collective-permute-start.1
  475.5 1.6 split.35
  477.1 1.7 collective-permute-done.1
  478.8 1.5 scatter-add.4
  480.3 2.7 fusion.71
  483.0 7.9 add_add_fusion.1
  492.3 6.8 fusion.25
  500.6 7.0 convolution_bitcast_fusion.2
  507.7 4.7 convolution_bitcast_fusion.3
  512.6 7.6 convolution_bitcast_fusion
  520.3 5.6 convolution_bitcast_fusion.1
  526.9 40.8 %all-reduce.15 = (f32[4,256]{1,0:T(4,128)}, f32[256]{0:T(256)}) all-reduce(f32[4,256]{1,0:T(4,128)S(1)} %pad_add_fusion.3, f32[256]{0:T(256)S(1)} %split.34), channel_id=1, replica_groups=mesh['seq'=16,'head'=2] {'seq','head'}, use_global_device_ids=true, to_apply=%region_34.35 | all-reduce | flops 1280 | bytes 10240 | tf_op jit(solution)/shard_map/psum | solution.py:210
  568.9 3.1 multiply_reduce_fusion.9
  571.9 77.5 %all-reduce.16 = (f32[768]{0:T(1024)}, f32[768,12]{0,1:T(8,128)}, f32[4,768]{1,0:T(4,128)}, f32[768]{0:T(1024)}, f32[12]{0:T(128)}, /*index=5*/f32[12]{0:T(128)}, f32[12]{0:T(128)}, f32[768]{0:T(1024)}) all-reduce(f32[768]{0:T(1024)S(1)} %get-tuple-element.303, ...), channel_id=1, replica_groups=mesh['seq'=16,'head'=2] {'seq'}, use_global_device_ids=true, to_apply=%region_24.25 | all-reduce | flops 14628 | bytes 117024 | tf_op jit(solution)/shard_map/psum | solution.py:194
  649.5 2.7 fusion.70
  652.2 7.8 all-reduce.24.cloned.1.call-done
  660.0 236.0 %all-reduce.26.cloned.1.call-done = (f32[768,768]{1,0:T(8,128)}, f32[768,768]{1,0:T(8,128)}, f32[768,768]{1,0:T(8,128)}) async-done(((f32[768,768]{1,0:T(8,128)}, f32[768,768]{1,0:T(8,128)}, f32[768,768]{1,0:T(8,128)}), (f32[768,768]{1,0:T(8,128)}, f32[768,768]{1,0:T(8,128)}, f32[768,768]{1,0:T(8,128)})) %all-reduce.26.cloned.1.call-update) | async-done | bytes 7077904 | tf_op jit(solution)/shard_map/psum | solution.py:194
  895.9 3.4 copy.239
  (275 shorter events, 72.8 us)
Async XLA Ops:
  7.2 226.8 %copy-start = (f32[768,768]{1,0:T(8,128)S(1)}, f32[768,768]{1,0:T(8,128)}, u32[]{:S(2)}) copy-start(f32[768,768]{1,0:T(8,128)} %param.24) | copy-start | bytes 7077892
  7.2 190.9 %all-gather.9.cloned.1.call-start = ((), (), s32[]{:S(2)}) async-start(), calls=%async_computation.5 | async-start | bytes 13369344 | tf_op jit(solution)/shard_map/all_gather | solution.py:23
  9.0 3.3 copy-start.19
  12.4 21.7 %copy-start.17 = (f32[2,256,256]{2,1,0:T(8,128)}, f32[2,256,256]{2,1,0:T(8,128)S(1)}, u32[]{:S(2)}) copy-start(f32[2,256,256]{2,1,0:T(8,128)S(1)} %fusion.73) | copy-start | bytes 1572868
  17.6 6.2 copy-start.66
  17.6 6.3 copy-start.56
  17.6 6.3 copy-start.60
  17.6 6.3 copy-start.37
  17.6 8.2 copy-start.57
  18.3 13.9 %collective-permute-start = (f32[2,3,1024]{2,1,0:T(4,128)}, f32[2,3,1024]{2,1,0:T(4,128)}, u32[]{:S(2)}, u32[]{:S(2)}) collective-permute-start(f32[2,3,1024]{2,1,0:T(4,128)} %fusion.117), channel_id=1, source_target_pairs={{0,2},{2,4},{4,6},{6,8},{8,10},{10,12},{12,14},{14,16},{16,18},{18... | collective-permute-start | bytes 73736 | tf_op jit(solution)/shard_map/ppermute | solution.py:18
  23.9 3.3 copy-start.62
  24.0 10.1 %copy-start.40 = (f32[1,1024]{1,0:T(1,128)}, f32[1,1024]{1,0:T(1,128)S(1)}, u32[]{:S(2)}) copy-start(f32[1,1024]{1,0:T(1,128)S(1)} %get-tuple-element.366) | copy-start | bytes 12292
  24.0 10.1 %copy-start.42 = (f32[1,1024]{1,0:T(1,128)}, f32[1,1024]{1,0:T(1,128)S(1)}, u32[]{:S(2)}) copy-start(f32[1,1024]{1,0:T(1,128)S(1)} %get-tuple-element.367) | copy-start | bytes 12292
  24.0 10.1 %copy-start.44 = (f32[1,1024]{1,0:T(1,128)}, f32[1,1024]{1,0:T(1,128)S(1)}, u32[]{:S(2)}) copy-start(f32[1,1024]{1,0:T(1,128)S(1)} %get-tuple-element.368) | copy-start | bytes 12292
  24.0 10.1 %copy-start.46 = (f32[1,1024]{1,0:T(1,128)}, f32[1,1024]{1,0:T(1,128)S(1)}, u32[]{:S(2)}) copy-start(f32[1,1024]{1,0:T(1,128)S(1)} %get-tuple-element.369) | copy-start | bytes 12292
  25.6 5.5 copy-start.61
  25.6 5.5 copy-start.64
  25.8 8.2 copy-start.20
  46.0 3.8 copy-start.59
  46.0 198.5 %all-gather.7.cloned.1.call-start = ((), (), s32[]{:S(2)}) async-start(), calls=%async_computation.2 | async-start | bytes 2359296 | tf_op jit(solution)/shard_map/all_gather | solution.py:163
  46.8 372.8 %all-gather.11.cloned.1.call-start = ((), (), s32[]{:S(2)}) async-start(), calls=%async_computation.6 | async-start | bytes 13369344 | tf_op jit(solution)/shard_map/all_gather | solution.py:23
  219.7 11.3 %copy-start.6 = (f32[2,12,64,128]{3,2,1,0:T(8,128)}, f32[2,12,64,128]{3,2,1,0:T(8,128)S(1)}, u32[]{:S(2)}) copy-start(f32[2,12,64,128]{3,2,1,0:T(8,128)S(1)} %get-tuple-element.254) | copy-start | bytes 2359300
  219.7 2.7 copy-start.11
  219.7 2.7 copy-start.35
  219.7 2.7 copy-start.38
  219.7 2.7 copy-start.48
  219.7 2.7 copy-start.49
  219.7 2.7 copy-start.65
  222.5 8.5 copy-start.22
  234.0 10.5 %copy-start.39 = (f32[768]{0:T(1024)S(1)}, f32[768]{0:T(1024)}, u32[]{:S(2)}) copy-start(f32[768]{0:T(1024)} %param.35) | copy-start | bytes 9220
  269.1 299.8 %all-reduce.22.cloned.1.call-start = ((), (), s32[]{:S(2)}) async-start(), calls=%async_computation.3 | async-start | bytes 3145728 | tf_op jit(solution)/shard_map/psum | solution.py:191
  303.6 4.3 copy-start.28
  307.9 5.1 copy-start.16
  419.6 22.1 %copy-start.7 = (f32[2,12,64,128]{3,2,1,0:T(8,128)S(1)}, f32[2,12,64,128]{3,2,1,0:T(8,128)}, u32[]{:S(2)}) copy-start(f32[2,12,64,128]{3,2,1,0:T(8,128)} %copy-done.6) | copy-start | bytes 2359300
  450.1 3.3 copy-start.21
  450.1 3.3 copy-start.55
  450.1 3.3 copy-start.58
  450.1 4.2 copy-start.31
  450.1 4.2 copy-start.32
  450.1 4.2 copy-start.33
  453.4 6.6 copy-start.27
  453.4 7.5 copy-start.63
  460.9 7.1 copy-start.5
  460.9 7.1 copy-start.18
  464.2 3.7 copy-start.29
  464.2 3.7 copy-start.30
  467.9 4.0 copy-start.41
  468.0 4.0 copy-start.43
  468.0 4.0 copy-start.45
  468.0 4.0 copy-start.47
  473.0 5.8 collective-permute-start.1
  477.1 3.2 copy-start.23
  480.3 2.7 copy-start.14
  490.9 158.5 %reduce-scatter.2.cloned.1.call-start = ((), (), s32[]{:S(2)}) async-start(), calls=%async_computation.1 | async-start | bytes 2359296 | tf_op jit(solution)/shard_map/reduce_scatter | solution.py:159
  499.2 160.8 %all-reduce.24.cloned.1.call-start = ((), (), s32[]{:S(2)}) async-start(), calls=%async_computation.4 | async-start | bytes 1572864 | tf_op jit(solution)/shard_map/psum | solution.py:210
  512.3 383.6 %all-reduce.26.cloned.1.call-start = ((), (), s32[]{:S(2)}) async-start(), calls=%async_computation.7 | async-start | bytes 14155776 | tf_op jit(solution)/shard_map/psum | solution.py:194
  512.6 7.7 copy-start.15
  525.9 42.8 %copy-start.67 = (f32[12]{0:T(128)S(1)}, f32[12]{0:T(128)}, u32[]{:S(2)}) copy-start(f32[12]{0:T(128)} %param.33) | copy-start | bytes 148
  568.8 3.1 copy-start.52
  568.8 80.6 %copy-start.51 = (f32[2,256]{1,0:T(2,128)S(1)}, f32[2,256]{1,0:T(2,128)}, u32[]{:S(2)}) copy-start(f32[2,256]{1,0:T(2,128)} %copy-done.50) | copy-start | bytes 6148
  568.8 80.6 %copy-start.24 = (f32[2,256,384]{2,1,0:T(8,128)S(1)}, f32[2,256,384]{2,1,0:T(8,128)}, u32[]{:S(2)}) copy-start(f32[2,256,384]{2,1,0:T(8,128)} %param.37) | copy-start | bytes 2359300
  895.9 3.4 copy-start.26
  899.3 3.0 copy-start.25
  901.0 2.8 copy-start.1
  (13 other events, 20.5 us)
Sparse Core Ops, SparseCore 0:
  46.2 151.8 all-gather.8
  199.6 7.9 all-gather.6
  269.2 150.3 all-gather.10
  491.0 20.3 all-reduce.21
  513.7 10.2 reduce-scatter.1
  529.5 130.3 all-reduce.23
  668.7 227.2 all-reduce.25
where the time goes:
time: 918 us; the launch traced here: 911 us
  waiting for transfers between devices  453 us (49%)
  blocking collectives  162 us (18%)
  matrix products  135 us (15%)
  other arithmetic  84.7 us (9%)
  local copies, waits for them, and re-layouts  50.2 us (5%)
  between operations  15.3 us (2%)
    psum x1, waiting for transfers between devices, body(): lax.psum((grad_w_gate, grad_w_inner, grad_w_step, grad_conv_inner, grad_b...  236 us
    all_gather x2, waiting for transfers between devices, entering_2(): everything = jax.tree.map(lambda part: lax.all_gather(part, axis), array)  207 us
    psum x1, blocking collectives, body(): lax.psum((grad_w_gate, grad_w_inner, grad_w_step, grad_conv_inner, grad_b...  77.5 us
    dot_general x15, matrix products, product(): return jnp.einsum('...k,kn->...n', left, right, precision=highest)  76 us
    select_n x32, other arithmetic, hop(): return jax.tree.map(lambda a, b: jnp.where(reached, a, b), new, before)  41.9 us
    psum x1, blocking collectives, body(): lax.psum((grad_w_state, grad_conv_state, grad_bias_state), ('seq', 'head'))  40.8 us
    all_gather x1, blocking collectives, entering_2(): everything = jax.tree.map(lambda part: lax.all_gather(part, axis), array)  38.9 us
    dot_general x3, matrix products, group_out(): within = jnp.einsum('shtr,srhp->sthp', mixing, inner_x, precision=highest)  30.1 us
  transfers between devices with their start and end apart: 9, of which 5 were waited for; matrix products, arithmetic and copies ran while one was open for 16% of the time, Pallas kernels for 0%

commit v1 on v0

v1 whole, which is shorter than its diff:
```python
import functools

import jax
import jax.numpy as jnp
from jax import lax
from jax.experimental import pallas as pl
from jax.experimental.pallas import tpu as pltpu
from jax.sharding import PartitionSpec as P

HEADS = 24
HEAD_DIM = 64
STATE = 128

highest = lax.Precision.HIGHEST
high = lax.Precision.HIGHEST
epsilon = 1e-05


def shifted(array, axis, by):
    length = lax.axis_size(axis)
    pairs = [(i, i + by) for i in range(length) if 0 <= i + by < length]
    return lax.ppermute(array, axis, pairs)


def scan_kernel(
    count, reverse, state_ref, decay_ref, out_ref,
    inbox, indecay, results, landed,
    send_a, recv_a, send_d, recv_d, send_b, recv_b,
):
    me = lax.axis_index("seq")
    barrier = pltpu.get_barrier_semaphore()

    def greet(d, carry):
        pl.semaphore_signal(
            barrier, inc=1, device_id={"seq": lax.rem(me + d, count)}, device_id_type=pl.DeviceIdType.MESH
        )
        return carry

    lax.fori_loop(1, count, greet, 0)
    pl.semaphore_wait(barrier, count - 1)

    def outward(d):
        to = lax.rem(me + d, count)
        return (
            pltpu.make_async_remote_copy(
                src_ref=state_ref.at[:, to], dst_ref=inbox.at[me], send_sem=send_a.at[d], recv_sem=recv_a.at[d],
                device_id={"seq": to}, device_id_type=pl.DeviceIdType.MESH,
            ),
            pltpu.make_async_remote_copy(
                src_ref=decay_ref, dst_ref=indecay.at[me], send_sem=send_d.at[d], recv_sem=recv_d.at[d],
                device_id={"seq": to}, device_id_type=pl.DeviceIdType.MESH,
            ),
        )

    def homeward(d):
        to = lax.rem(me + d, count)
        return pltpu.make_async_remote_copy(
            src_ref=results.at[to], dst_ref=landed.at[:, me], send_sem=send_b.at[d], recv_sem=recv_b.at[d],
            device_id={"seq": to}, device_id_type=pl.DeviceIdType.MESH,
        )

    def start_out(d, carry):
        for copy in outward(d):
            copy.start()
        return carry

    def wait_out(d, carry):
        for copy in outward(d):
            copy.wait()
        return carry

    def start_home(d, carry):
        homeward(d).start()
        return carry

    def wait_home(d, carry):
        homeward(d).wait()
        return carry

    lax.fori_loop(1, count, start_out, 0)
    inbox[pl.ds(me, 1)] = state_ref[:, pl.ds(me, 1)].reshape((1,) + inbox.shape[1:])
    indecay[pl.ds(me, 1)] = decay_ref[...][None]
    lax.fori_loop(1, count, wait_out, 0)

    for s in range(inbox.shape[1]):

        def hop(k, running):
            at = count - 1 - k if reverse else k
            results[at, s] = running
            return running * indecay[at, s : s + 1, :] + inbox[at, s]

        lax.fori_loop(0, count, hop, jnp.zeros(inbox.shape[2:], jnp.float32))
    lax.fori_loop(1, count, start_home, 0)
    landed[:, pl.ds(me, 1)] = results[pl.ds(me, 1)].reshape(
        (landed.shape[0], 1) + landed.shape[2:]
    )
    lax.fori_loop(1, count, wait_home, 0)
    out_ref[...] = landed[...]


def pass_states(state, decay, reverse):
    count = lax.axis_size("seq")
    seqs, depth, width = state.shape
    rows = depth // count
    parts = state.reshape(seqs, count, rows, width)
    spread = jnp.repeat(decay, HEAD_DIM, axis=-1)
    vmem = pl.BlockSpec(memory_space=pltpu.VMEM)
    boxes = (count, seqs, rows, width)
    sems = pltpu.SemaphoreType.DMA((count,))
    entering = pl.pallas_call(
        functools.partial(scan_kernel, count, reverse),
        out_shape=jax.ShapeDtypeStruct(parts.shape, jnp.float32),
        in_specs=[vmem, vmem],
        out_specs=vmem,
        scratch_shapes=[
            pltpu.VMEM(boxes, jnp.float32),
            pltpu.VMEM((count, seqs, width), jnp.float32),
            pltpu.VMEM(boxes, jnp.float32),
            pltpu.VMEM(parts.shape, jnp.float32),
            sems, sems, sems, sems, sems, sems,
        ],
        compiler_params=pltpu.CompilerParams(
            collective_id=1 if reverse else 0, has_side_effects=True, vmem_limit_bytes=40 * 2**20
        ),
        name="states_back" if reverse else "states_on",
    )(parts, spread)
    return entering.reshape(state.shape)


def product(left, right):
    return jnp.einsum("...k,kn->...n", left, right, precision=high)


def project(hidden, w_gate, w_inner, w_state, w_step):
    mixed_in = jnp.concatenate([product(hidden, w_inner), product(hidden, w_state)], axis=-1)
    return (product(hidden, w_gate), mixed_in, product(hidden, w_step))


def convolve(
    mixed_in, before, conv_inner, conv_state, bias_inner, bias_state, raw_step, step_bias, decay_log
):
    weights = jnp.concatenate([conv_inner, conv_state], axis=-1)
    summed = jnp.concatenate([bias_inner, bias_state], axis=-1) + jnp.zeros_like(mixed_in)
    padded = jnp.concatenate([before, mixed_in], axis=1)
    length = mixed_in.shape[1]
    for offset in range(weights.shape[0]):
        summed = summed + weights[offset] * padded[:, offset : offset + length]
    step_size = jax.nn.softplus(raw_step + step_bias)
    lower = jnp.tril(jnp.ones((length, length), jnp.float32))
    cumulative = jnp.einsum(
        "tr,srh->sth", lower, -jnp.exp(decay_log) * step_size, precision=highest
    )
    return (jax.nn.silu(summed), step_size, cumulative)


def unpack(active):
    inner_width = active.shape[-1] - 2 * STATE
    return (
        active[..., :inner_width],
        active[..., inner_width : inner_width + STATE],
        active[..., inner_width + STATE :],
    )


def by_channel(per_head):
    return jnp.repeat(per_head, HEAD_DIM, axis=-1)


def end_state(active, step_size, cumulative):
    inner_x, input_map, output_map = unpack(active)
    weight_end = jnp.exp(cumulative[:, -1:, :] - cumulative) * step_size
    local_state = jnp.einsum(
        "sln,slc->snc", input_map, inner_x * by_channel(weight_end), precision=highest
    )
    return (local_state, jnp.exp(cumulative[:, -1, :]))


def group_within(active, step_size, cumulative, skip_gain):
    inner_x, input_map, output_map = unpack(active)
    length = active.shape[1]
    scores = jnp.einsum("stn,srn->str", output_map, input_map, precision=high)
    by_head = jnp.transpose(cumulative, (0, 2, 1))
    causal = (jnp.arange(length)[:, None] >= jnp.arange(length)[None, :])[None, None]
    spread = by_head[:, :, :, None] - by_head[:, :, None, :]
    decays = jnp.where(causal, jnp.exp(jnp.where(causal, spread, 0.0)), 0.0)
    mixing = scores[:, None] * decays * jnp.transpose(step_size, (0, 2, 1))[:, :, None, :]
    heads = inner_x.reshape(inner_x.shape[:2] + (-1, HEAD_DIM))
    within = jnp.einsum("shtr,srhp->sthp", mixing, heads, precision=high)
    return within.reshape(inner_x.shape) + by_channel(skip_gain) * inner_x


def group_out(active, step_size, cumulative, entering, gate_proj, skip_gain):
    within = group_within(active, step_size, cumulative, skip_gain)
    output_map = unpack(active)[2]
    across = by_channel(jnp.exp(cumulative)) * jnp.einsum(
        "stn,snc->stc", output_map, entering, precision=highest
    )
    gated_out = (within + across) * jax.nn.silu(gate_proj)
    return (gated_out, jnp.sum(gated_out * gated_out, axis=-1))


def finish(gated_out, square_sum, out_gain, w_out):
    inverse = lax.rsqrt(square_sum / (HEADS * HEAD_DIM) + epsilon)
    return product(gated_out * inverse[..., None] * out_gain, w_out)


def after(array, earlier):
    return lax.optimization_barrier((array, earlier))


def body(
    tokens,
    norm_gain,
    w_gate,
    w_inner,
    w_state,
    w_step,
    conv_inner,
    conv_state,
    bias_inner,
    bias_state,
    step_bias,
    decay_log,
    skip_gain,
    out_gain,
    w_out,
    cotangent,
):
    width = tokens.shape[-1]
    full_cot = lax.all_gather(cotangent, "head", axis=2, tiled=True)
    inverse = lax.rsqrt(jnp.mean(tokens * tokens, axis=-1, keepdims=True) + epsilon)
    scaled = tokens * inverse
    hidden = scaled * norm_gain
    gate_proj, mixed_in, raw_step = project(hidden, w_gate, w_inner, w_state, w_step)
    edge_rows = conv_inner.shape[0] - 1
    before = shifted(mixed_in[:, mixed_in.shape[1] - edge_rows :], "seq", 1)
    (active, step_size, cumulative), convolve_back = jax.vjp(
        convolve,
        mixed_in,
        before,
        conv_inner,
        conv_state,
        bias_inner,
        bias_state,
        raw_step,
        step_bias,
        decay_log,
    )
    (local_state, decay_all), state_back = jax.vjp(end_state, active, step_size, cumulative)
    entering = pass_states(local_state, decay_all, False)
    (gated_out, partial_sq), group_back = jax.vjp(
        group_out, active, step_size, cumulative, entering, gate_proj, skip_gain
    )
    square_sum = lax.psum(partial_sq, "head")
    partial_out, finish_back = jax.vjp(finish, gated_out, square_sum, out_gain, w_out)
    shared_out = lax.psum_scatter(partial_out, "head", scatter_dimension=2, tiled=True)
    columns = shared_out.shape[2]
    col_start = lax.axis_index("head") * columns
    my_tokens = lax.dynamic_slice_in_dim(tokens, col_start, columns, 2)
    result = my_tokens + shared_out
    grad_gated, grad_square, grad_out_gain, grad_w_out = finish_back(full_cot)
    grad_partial_sq = lax.psum(grad_square, "head")
    grad_active, grad_step, grad_cumul, grad_entering, grad_gate, grad_skip_gain = group_back(
        (grad_gated, grad_partial_sq)
    )
    grad_w_gate = jnp.einsum("stk,stn->kn", hidden, grad_gate, precision=high)
    early = jnp.concatenate([grad_w_gate, grad_w_out], axis=0)
    grad_entering, early = after(grad_entering, early)
    sum_early = lax.psum(early, "seq")
    carried = pass_states(grad_entering, decay_all, True)
    grad_decay = jnp.sum(carried * entering, axis=1)
    grad_decay = jnp.sum(grad_decay.reshape(grad_decay.shape[0], -1, HEAD_DIM), axis=-1)
    more_active, more_step, more_cumul = state_back((carried, grad_decay))
    (
        grad_mixed,
        grad_before,
        grad_conv_inner,
        grad_conv_state,
        grad_bias_inner,
        grad_bias_state,
        grad_raw,
        grad_step_bias,
        grad_decay_log,
    ) = convolve_back((grad_active + more_active, grad_step + more_step, grad_cumul + more_cumul))
    returned = shifted(grad_before, "seq", -1)
    grad_mixed = grad_mixed.at[:, grad_mixed.shape[1] - edge_rows :].add(returned)
    grad_inner = grad_mixed[..., : w_inner.shape[1]]
    grad_maps = grad_mixed[..., w_inner.shape[1] :]
    grad_w_inner = jnp.einsum("stk,stn->kn", hidden, grad_inner, precision=high)
    grad_maps_t = jnp.einsum("stn,stk->nk", grad_maps, hidden, precision=high)
    grad_step_t = jnp.einsum("stn,stk->nk", grad_raw, hidden, precision=high)
    grad_hidden = (
        jnp.einsum("stn,kn->stk", grad_gate, w_gate, precision=high)
        + jnp.einsum("stn,kn->stk", grad_inner, w_inner, precision=high)
        + jnp.einsum("stn,kn->stk", grad_maps, w_state, precision=high)
        + jnp.einsum("stn,kn->stk", grad_raw, w_step, precision=high)
    )

    maps = w_state.shape[1]
    taps = conv_state.shape[0]
    loose = jnp.concatenate([grad_conv_state.reshape(-1), grad_bias_state])
    loose_rows = -(-loose.size // width)
    shared_rows = maps + 1 + loose_rows
    fill = -shared_rows % 16
    shared = jnp.concatenate(
        [
            grad_maps_t,
            jnp.sum(grad_hidden * scaled, axis=(0, 1))[None],
            jnp.pad(loose, (0, loose_rows * width - loose.size)).reshape(loose_rows, width),
            jnp.zeros((fill, width), jnp.float32),
        ],
        axis=0,
    )
    shared = lax.psum_scatter(shared, "head", scatter_dimension=0, tiled=True)
    small = jnp.concatenate([grad_step_bias, grad_decay_log, grad_skip_gain])
    heads = step_bias.shape[0]
    channels = w_inner.shape[1]
    packed = jnp.concatenate(
        [
            grad_conv_inner,
            grad_bias_inner[None],
            grad_out_gain[None],
            jnp.pad(small, (0, channels - small.size))[None],
        ],
        axis=0,
    )
    packed = jnp.concatenate([grad_w_inner, shared, grad_step_t, packed], axis=0)
    packed, sum_early = after(packed, sum_early)
    total = lax.psum(packed, "seq")

    my_hidden = lax.psum_scatter(grad_hidden, "head", scatter_dimension=2, tiled=True)
    along = lax.psum(jnp.sum(grad_hidden * hidden, axis=-1), "head")[..., None]
    my_gain = lax.dynamic_slice_in_dim(norm_gain, col_start, columns, 0)
    grad_tokens = (
        cotangent + inverse * my_gain * my_hidden - my_tokens * (inverse * inverse * along / width)
    )

    at = 0

    def take(rows):
        nonlocal at
        at += rows
        return total[at - rows : at]

    sum_w_inner = take(width)
    sum_shared = lax.all_gather(take(shared.shape[0]), "head", axis=0, tiled=True)
    sum_w_step = take(heads).T
    sum_conv_inner = take(taps)
    sum_bias_inner = take(1)[0]
    sum_out_gain = take(1)[0]
    sums = take(1)[0]
    loose = sum_shared[maps + 1 : shared_rows].reshape(-1)
    sum_conv_state = loose[: taps * maps].reshape(taps, maps)
    sum_bias_state = loose[taps * maps : (taps + 1) * maps]
    return (
        result,
        grad_tokens,
        sum_shared[maps],
        sum_early[:width],
        sum_w_inner,
        sum_shared[:maps].T,
        sum_w_step,
        sum_conv_inner,
        sum_conv_state,
        sum_bias_inner,
        sum_bias_state,
        sums[:heads],
        sums[heads : 2 * heads],
        sums[2 * heads : 3 * heads],
        sum_out_gain,
        sum_early[width:],
    )


def solution(mesh):
    return jax.shard_map(
        body,
        mesh=mesh,
        in_specs=(
            P(None, "seq", None),
            P(),
            P(None, "head"),
            P(None, "head"),
            P(),
            P(None, "head"),
            P(None, "head"),
            P(),
            P("head"),
            P(),
            P("head"),
            P("head"),
            P("head"),
            P("head"),
            P("head", None),
            P(None, "seq", "head"),
        ),
        out_specs=(
            P(None, "seq", "head"),
            P(None, "seq", "head"),
            P(),
            P(None, "head"),
            P(None, "head"),
            P(),
            P(None, "head"),
            P(None, "head"),
            P(),
            P("head"),
            P(),
            P("head"),
            P("head"),
            P("head"),
            P("head"),
            P("head", None),
        ),
        check_vma=False,
    )
```

time: 918 us -> 693 us (0.75)
  blocking collectives: 162 us -> 10.2 us
  waiting for transfers between devices: 453 us -> 340 us
  Pallas kernels: 0 us -> 83.1 us
  other arithmetic: 84.7 us -> 44 us
  local copies, waits for them, and re-layouts: 50.2 us -> 71.9 us
  matrix products: 135 us -> 116 us
    all_gather x2 -> x0, waiting for transfers between devices: 207 us -> none  [entering_2(): everything = jax.tree.map(lambda part: lax.all_gather(part, axis), array)]
    psum x2 -> x1, blocking collectives: 118 us -> 2.44 us  [body(): along = lax.psum(jnp.sum(grad_hidden * hidden, axis=-1), 'head')[..., None]]
    pallas_call x0 -> x2, Pallas kernels: none -> 83.1 us  [pass_states(): pl.pallas_call(functools.partial(scan_kernel, count, reverse), out_shape=...]
    psum x3 -> x2, waiting for transfers between devices: 244 us -> 314 us  [the longest x1 172 us: body(): sum_early = lax.psum(early, 'seq')]
    select_n x32 -> x1, other arithmetic: 41.9 us -> 1.29 us  [convolve(): step_size = jax.nn.softplus(raw_step + step_bias)]
    all_gather x1, blocking collectives: 38.9 us -> 2.4 us  [body(): lax.all_gather(take(shared.shape[0]), 'head', axis=0, tiled=True)]
    dot_general x27 -> x29, matrix products: 135 us -> 116 us  [the longest x7 35.1 us: product(): return jnp.einsum('...k,kn->...n', left, right, precision=high)]
    reduce_scatter x0 -> x2, waiting for transfers between devices: none -> 13.1 us  [the longest x1 13.1 us: body(): lax.psum_scatter(grad_hidden, 'head', scatter_dimension=2, tiled=True)]
  transfers between devices with their start and end apart: 9 -> 8, of which waited for: 5 -> 5; matrix products, arithmetic and copies ran while one was open for 16% -> 14% of each run, Pallas kernels for 0% -> 6%
where the time goes in v1:
time: 693 us; the launch traced here: 688 us
  waiting for transfers between devices  340 us (49%)
  matrix products  116 us (17%)
  Pallas kernels  83.1 us (12%)
  local copies, waits for them, and re-layouts  71.9 us (10%)
  other arithmetic  44 us (6%)
  between operations  15.3 us (2%)
  blocking collectives  10.2 us (1%)
  starting transfers between devices  7.67 us (1%)
    psum x1, waiting for transfers between devices, body(): sum_early = lax.psum(early, 'seq')  172 us
    psum x1, waiting for transfers between devices, body(): total = lax.psum(packed, 'seq')  142 us
    pallas_call x2, Pallas kernels, pass_states(): pl.pallas_call(functools.partial(scan_kernel, count, reverse), out_shape=...  83.1 us
    dot_general x7, matrix products, product(): return jnp.einsum('...k,kn->...n', left, right, precision=high)  35.1 us
    dot_general x3, matrix products, group_within(): within = jnp.einsum('shtr,srhp->sthp', mixing, heads, precision=high)  26.9 us
  transfers between devices with their start and end apart: 8, of which 5 were waited for; matrix products, arithmetic and copies ran while one was open for 14% of the time, Pallas kernels for 6%

profile of v1, /device:TPU:0, one launch (start us, length us, event | category | flops | bytes accessed | tf_op | source)
XLA Modules:
  0.0 687.8 jit_solution(18316567657116015510)
XLA Ops:
  8.0 1.7 multiply_reduce_fusion.12
  9.9 2.8 fusion.54
  12.7 4.1 fusion.31
  18.6 5.9 collective-permute-start
  25.2 1.6 fusion.101
  30.5 2.0 fusion.106
  34.0 1.7 copy.152
  39.2 3.0 copy.159
  43.5 3.1 copy.157
  47.3 1.8 maximum_maximum_fusion
  49.2 2.5 fusion.35
  54.3 3.1 copy.149
  57.4 9.7 %fusion.5 = f32[2,12,64,256]{3,2,1,0:T(8,128)} fusion(f32[2,256,12,64]{1,3,2,0:T(8,128)} %bitcast.175, f32[2,12,256]{2,1,0:T(8,128)S(1)} %copy-done.55, f32[2,12,256]{2,1,0:T(8,128)S(1)} %fusion.80, f32[2,256,256]{2,1,0:T(8,128)S(1)} %fusion.90, pred[256,256]{1,0:T(8,128)(4,1)S(1)} %copy-done.52), kind=kOutput, calls=%fused_computation.8 | convolution fusion | flops 1215823872 | bytes 3784704 | tf_op jit(solution)/shard_map/jvp(shtr,srhp->sthp)/dot_general | solution.py:188
  67.1 3.0 copy.153
  70.1 3.2 convolution_bitcast_fusion.3.state_ref
  73.3 41.3 %states_on.1 = f32[2,16,8,768]{3,2,1,0:T(8,128)S(1)} custom-call(f32[2,16,8,768]{3,2,1,0:T(8,128)S(1)} %convolution_bitcast_fusion.3.state_ref, f32[2,768]{1,0:T(2,128)S(1)} %reshape.227.decay_ref), custom_call_target="tpu_custom_call" | custom-call | tf_op jit(solution)/shard_map/states_on/pallas_call | solution.py:110
  116.1 6.8 multiply_reduce_fusion.11
  122.9 2.4 psum.35
  125.3 7.9 %multiply_reduce_fusion.7 = (f32[768]{0:T(1024)S(1)}, f32[2,256]{1,0:T(2,128)S(1)}, f32[2,256,768]{2,1,0:T(8,128)}) fusion(f32[2,256,768]{2,1,0:T(8,128)} %get-tuple-element.158, f32[2,256]{1,0:T(2,128)S(1)} %fusion.107, f32[768]{0:T(1024)S(1)} %copy-done.54, f32[2,256,768]{2,1,0:T(8,128)} %all-gather.2.cloned.1.call-done, f32[768,768]{1,0:T(8,128)} %param.32), kind=kOutput, calls=%fused_computation.59 | convolution fusion | flops 3626236672 | bytes 7088128 | tf_op jit(solution)/shard_map/transpose(jvp(...k,kn->...n))/dot_general | solution.py:131
  133.3 2.9 psum.36
  136.1 4.5 multiply_reduce_fusion.6
  140.7 2.3 fusion.49
  142.9 2.9 fusion.60
  145.9 5.2 fusion.25
  151.0 4.8 convolution_bitcast_fusion.2
  155.8 4.6 convolution_bitcast_fusion.1
  160.4 2.4 pad_maximum_fusion
  162.9 41.8 %states_back.1 = f32[2,16,8,768]{3,2,1,0:T(8,128)S(1)} custom-call(f32[2,16,8,768]{3,2,1,0:T(8,128)S(1)} %bitcast.167, f32[2,768]{1,0:T(2,128)S(1)} %reshape.227.decay_ref), custom_call_target="tpu_custom_call" | custom-call | tf_op jit(solution)/shard_map/states_back/pallas_call | solution.py:110
  204.8 3.1 fusion.47
  207.9 3.3 fusion.122
  211.3 3.2 copy.161
  214.5 11.6 %fusion.8 = (f32[2,12,256]{2,1,0:T(8,128)S(1)}, f32[2,12,256]{2,1,0:T(8,128)S(1)}, f32[2,12,256]{2,1,0:T(8,128)S(1)}, f32[2,256,256]{2,1,0:T(8,128)S(1)}) fusion(f32[2,12,256]{2,1,0:T(8,128)S(1)} %copy-done.56, f32[2,12,256]{2,1,0:T(8,128)S(1)} %fusion.80, f32[2,256,256]{2,1,0:T(8,128)S(1)} %copy-done.49, pred[256,256]{1,0:T(8,128)(4,1)S(1)} %copy-done.53, ...), kind=kOutput, calls=%fused_computation.11 | convolution fusion | flops 1231403008 | bytes 4382720 | tf_op jit(solution)/shard_map/transpose(jvp(shtr,srhp->sthp))/dot_general | solution.py:188
  226.2 5.6 fusion.3
  231.8 2.0 fusion.93
  233.8 1.6 fusion.87
  235.3 1.6 copy.163
  237.0 4.0 multiply_add_fusion.1
  241.8 3.3 multiply_reduce_fusion.5
  249.5 2.4 pad_add_fusion
  252.1 3.0 copy.169
  255.1 1.7 reduce_sum.223
  260.3 1.6 copy.171
  262.0 1.6 reduce_sum.224
  265.6 3.2 fusion.115
  269.8 2.6 fusion.102
  273.8 1.7 split.27
  275.5 2.7 collective-permute-done.1
  279.2 1.7 scatter-add.4
  280.8 2.9 convolution_bitcast_fusion.4
  283.8 5.9 fusion.29
  289.7 3.2 multiply_reduce_fusion.8
  294.7 7.4 %fusion.23 = f32[2,256,768]{2,1,0:T(8,128)} fusion(f32[768,768]{1,0:T(8,128)} %param.32, f32[2,256,768]{2,1,0:T(8,128)} %get-tuple-element.158, f32[768]{0:T(1024)S(1)} %copy-done.54, f32[2,256]{1,0:T(2,128)S(1)} %fusion.107), kind=kOutput, calls=%fused_computation.31 | convolution fusion | flops 3624665088 | bytes 5510144 | tf_op jit(solution)/shard_map/jvp(...k,kn->...n)/dot_general | solution.py:131
  304.3 7.1 %convolution_bitcast_fusion = f32[768,768]{1,0:T(8,128)} fusion(f32[2,256,1024]{2,1,0:T(8,128)} %scatter-add.4, f32[2,256,768]{2,1,0:T(8,128)S(1)} %copy-done.6, f32[768]{0:T(1024)S(1)} %copy-done.50, f32[2,256]{1,0:T(2,128)S(1)} %add_rsqrt_fusion), kind=kOutput, calls=%fused_computation.53 | convolution fusion | flops 3624665088 | bytes 5510144 | tf_op jit(solution)/shard_map/stk,stn->kn/dot_general | solution.py:289
  311.4 10.7 %concatenate.37 = f32[923,768]{1,0:T(8,128)} concatenate(f32[768,768]{1,0:T(8,128)} %convolution_bitcast_fusion, f32[136,768]{1,0:T(8,128)} %reduce-scatter.8.cloned.1.call-done, f32[12,768]{1,0:T(8,128)S(1)} %convolution_bitcast_fusion.5, f32[4,768]{1,0:T(4,128)S(1)} %pad_add_fusion.2, f32[1,768]{1,0:T(1,128)S(1)} %broadcast_in_dim.107, f32[1,768]{1,0:T(1,128)S(1)} %broadcast_in_dim.108, ...), dimensions={0} | concatenate | bytes 5670912 | tf_op jit(solution)/shard_map/concatenate | solution.py:327
  322.1 172.4 %all-reduce.21.cloned.1.call-done = f32[1536,768]{1,0:T(8,128)} async-done(((f32[1536,768]{1,0:T(8,128)}), f32[1536,768]{1,0:T(8,128)}) %all-reduce.21.cloned.1.call-update) | async-done | bytes 4718608 | tf_op jit(solution)/shard_map/psum | solution.py:269
  494.6 2.4 psum.37
  497.1 7.6 %reduce-scatter.4.cloned.1.call-done = f32[2,256,384]{2,1,0:T(8,128)} async-done(((f32[2,256,768]{2,1,0:T(8,128)}), f32[2,256,384]{2,1,0:T(8,128)}) %reduce-scatter.4.cloned.1.call-update) | async-done | bytes 786448 | tf_op jit(solution)/shard_map/reduce_scatter | solution.py:256
  504.7 13.1 %reduce-scatter.6.cloned.1.call-done = f32[2,256,384]{2,1,0:T(8,128)} async-done(((f32[2,256,768]{2,1,0:T(8,128)}), f32[2,256,384]{2,1,0:T(8,128)}) %reduce-scatter.6.cloned.1.call-update) | async-done | bytes 786448 | tf_op jit(solution)/shard_map/reduce_scatter | solution.py:331
  517.8 2.9 multiply_subtract_fusion
  520.9 2.5 fusion.121
  523.4 142.0 %all-reduce.23.cloned.1.call-done = f32[923,768]{1,0:T(8,128)} async-done(((f32[923,768]{1,0:T(8,128)}), f32[923,768]{1,0:T(8,128)}) %all-reduce.23.cloned.1.call-update) | async-done | bytes 2835472 | tf_op jit(solution)/shard_map/psum | solution.py:329
  666.4 2.4 all_gather.7
  676.0 1.6 slice_bitcast_fusion.1
  677.5 3.2 slice.189
  (237 shorter events, 44.9 us)
Async XLA Ops:
  7.2 108.9 %copy-start = (f32[768,768]{1,0:T(8,128)S(1)}, f32[768,768]{1,0:T(8,128)}, u32[]{:S(2)}) copy-start(f32[768,768]{1,0:T(8,128)} %param.20) | copy-start | bytes 7077892
  7.2 2.5 copy-start.50
  7.2 118.1 %all-gather.2.cloned.1.call-start = ((), (), s32[]{:S(2)}) async-start(), calls=%async_computation.4 | async-start | bytes 2359296 | tf_op jit(solution)/shard_map/all_gather | solution.py:230
  7.9 303.4 %reduce-scatter.8.cloned.1.call-start = ((), (), s32[]{:S(2)}) async-start(), calls=%async_computation.6 | async-start | bytes 1253376 | tf_op jit(solution)/shard_map/reduce_scatter | solution.py:314
  9.7 2.9 copy-start.30
  12.6 36.5 %copy-start.28 = (f32[2,256,256]{2,1,0:T(8,128)}, f32[2,256,256]{2,1,0:T(8,128)S(1)}, u32[]{:S(2)}) copy-start(f32[2,256,256]{2,1,0:T(8,128)S(1)} %fusion.54) | copy-start | bytes 1572868
  17.9 7.2 %copy-start.70 = (f32[12]{0:T(128)S(1)}, f32[12]{0:T(128)}, u32[]{:S(2)}) copy-start(f32[12]{0:T(128)} %param.29) | copy-start | bytes 148
  17.9 7.2 %copy-start.51 = (f32[768,12]{0,1:T(8,128)S(1)}, f32[768,12]{0,1:T(8,128)}, u32[]{:S(2)}) copy-start(f32[768,12]{0,1:T(8,128)} %param.23) | copy-start | bytes 110596
  17.9 9.1 %copy-start.61 = (f32[12]{0:T(128)S(1)}, f32[12]{0:T(128)}, u32[]{:S(2)}) copy-start(f32[12]{0:T(128)} %param.28) | copy-start | bytes 148
  18.6 28.8 %collective-permute-start = (f32[2,3,1024]{2,1,0:T(4,128)}, f32[2,3,1024]{2,1,0:T(4,128)}, u32[]{:S(2)}, u32[]{:S(2)}) collective-permute-start(f32[2,3,1024]{2,1,0:T(4,128)} %fusion.105), channel_id=1, source_target_pairs={{0,2},{2,4},{4,6},{6,8},{8,10},{10,12},{12,14},{14,16},{16,18},{18... | collective-permute-start | bytes 73736 | tf_op jit(solution)/shard_map/ppermute | solution.py:22
  25.2 4.5 copy-start.67
  25.2 5.2 copy-start.59
  25.2 5.2 copy-start.63
  27.0 8.7 %copy-start.39 = (f32[2,256,12]{2,0,1:T(2,128)}, f32[2,256,12]{2,0,1:T(2,128)S(1)}, u32[]{:S(2)}) copy-start(f32[2,256,12]{2,0,1:T(2,128)S(1)} %copy.150) | copy-start | bytes 73732
  27.0 5.5 copy-start.64
  30.4 2.8 copy-start.57
  49.1 2.5 copy-start.7
  53.0 4.4 copy-start.48
  54.3 3.1 copy-start.52
  54.3 3.1 copy-start.55
  70.1 44.5 %copy-start.10 = (f32[2,256,1024]{2,1,0:T(8,128)S(1)}, f32[2,256,1024]{2,1,0:T(8,128)}, u32[]{:S(2)}) copy-start(f32[2,256,1024]{2,1,0:T(8,128)} %copy-done.9) | copy-start | bytes 6291460
  70.1 45.9 %copy-start.36 = (f32[2,256,768]{2,1,0:T(8,128)S(1)}, f32[2,256,768]{2,1,0:T(8,128)}, u32[]{:S(2)}) copy-start(f32[2,256,768]{2,1,0:T(8,128)} %copy.153) | copy-start | bytes 4718596
  73.3 42.7 %copy-start.24 = (f32[2,256,768]{2,1,0:T(8,128)S(1)}, f32[2,256,768]{2,1,0:T(8,128)}, u32[]{:S(2)}) copy-start(f32[2,256,768]{2,1,0:T(8,128)} %copy.159) | copy-start | bytes 4718596
  116.1 6.8 copy-start.27
  116.1 9.2 %copy-start.54 = (f32[768]{0:T(1024)S(1)}, f32[768]{0:T(1024)}, u32[]{:S(2)}) copy-start(f32[768]{0:T(1024)} %param.31) | copy-start | bytes 9220
  136.1 4.5 copy-start.25
  140.6 2.3 copy-start.12
  145.8 5.2 copy-start.5
  151.0 4.8 copy-start.13
  151.0 4.8 copy-start.37
  160.4 2.4 copy-start.2
  162.9 42.0 %copy-start.11 = (f32[2,256,1024]{2,1,0:T(8,128)S(1)}, f32[2,256,1024]{2,1,0:T(8,128)}, u32[]{:S(2)}) copy-start(f32[2,256,1024]{2,1,0:T(8,128)} %copy-done.9) | copy-start | bytes 6291460
  204.8 3.1 copy-start.23
  211.3 3.2 copy-start.44
  211.3 3.2 copy-start.49
  211.3 3.2 copy-start.53
  211.3 3.2 copy-start.56
  214.5 11.7 %copy-start.45 = (f32[2,256,768]{1,2,0:T(8,128)S(1)}, f32[2,256,768]{1,2,0:T(8,128)}, u32[]{:S(2)}) copy-start(f32[2,256,768]{1,2,0:T(8,128)} %copy.161) | copy-start | bytes 4718596
  237.0 4.0 copy-start.8
  237.0 4.0 copy-start.16
  237.0 4.0 copy-start.29
  237.0 4.9 copy-start.32
  237.0 4.9 copy-start.46
  246.2 2.7 copy-start.21
  246.2 3.4 copy-start.22
  255.1 5.2 copy-start.34
  265.6 8.2 %copy-start.65 = (f32[1,1,256]{2,1,0:T(1,128)S(1)}, f32[1,1,256]{2,1,0:T(1,128)}, u32[]{:S(2)}) copy-start(f32[1,1,256]{2,1,0:T(1,128)} %split.28) | copy-start | bytes 3076
  265.6 8.2 %copy-start.31 = (f32[2,259,1024]{2,1,0:T(8,128)S(1)}, f32[2,259,1024]{2,1,0:T(8,128)}, u32[]{:S(2)}) copy-start(f32[2,259,1024]{2,1,0:T(8,128)} %pad_add_fusion) | copy-start | bytes 6365188
  272.4 5.8 collective-permute-start.1
  273.8 4.5 copy-start.18
  273.8 4.5 copy-start.20
  275.5 5.3 copy-start.6
  280.8 2.9 copy-start.26
  283.7 5.9 copy-start.33
  283.7 5.9 copy-start.35
  283.7 5.9 copy-start.42
  289.7 3.2 copy-start.60
  293.9 200.6 %all-reduce.21.cloned.1.call-start = ((), (), s32[]{:S(2)}) async-start(), calls=%async_computation.7 | async-start | bytes 9437184 | tf_op jit(solution)/shard_map/psum | solution.py:269
  294.6 210.1 %reduce-scatter.4.cloned.1.call-start = ((), (), s32[]{:S(2)}) async-start(), calls=%async_computation.3 | async-start | bytes 2359296 | tf_op jit(solution)/shard_map/reduce_scatter | solution.py:256
  302.1 215.7 %reduce-scatter.6.cloned.1.call-start = ((), (), s32[]{:S(2)}) async-start(), calls=%async_computation.5 | async-start | bytes 2359296 | tf_op jit(solution)/shard_map/reduce_scatter | solution.py:331
  302.7 362.7 %all-reduce.23.cloned.1.call-start = ((), (), s32[]{:S(2)}) async-start(), calls=%async_computation.8 | async-start | bytes 5701632 | tf_op jit(solution)/shard_map/psum | solution.py:329
  322.1 195.7 %copy-start.43 = (f32[2,256,384]{2,1,0:T(8,128)S(1)}, f32[2,256,384]{2,1,0:T(8,128)}, u32[]{:S(2)}) copy-start(f32[2,256,384]{2,1,0:T(8,128)} %param.33) | copy-start | bytes 2359300
  517.8 3.1 copy-start.38
  676.0 4.8 copy-start.1
  (16 other events, 25.7 us)
Sparse Core Ops, SparseCore 0:
  9.6 12.4 all-gather.1
  294.0 12.8 reduce-scatter.7
  313.6 180.9 all-reduce.20
  496.6 8.0 reduce-scatter.3
  507.5 10.2 reduce-scatter.5
  523.4 141.9 all-reduce.22
